TPU v7x, 512 devices: a whole 4x8x8 slice. The times are simulated.
512 devices in a mesh: ep: 64 (over y, z), dp: 8 (over x, core).
Axes of the slice: x: 4, y: 8, z: 8, core: 2. Of those that a mesh axis runs over, the one named last changes fastest.
Arguments:
- tokens: bfloat16 [8192, 4096], P('ep', 'dp'), may hold values from -6 to 6
- routing: int32 [8192, 8], P('ep'), may hold values from 0 to 255, all different within a row; in each aligned block of 128 rows (0 to 127, 128 to 255, ...) at most 8 rows name the same one
- w_gate: bfloat16 [64, 4096, 1024], P('ep', 'dp'), may hold values from -0.09375 to 0.09375
- w_up: bfloat16 [64, 4096, 1024], P('ep', 'dp'), may hold values from -0.09375 to 0.09375
- cotangent: bfloat16 [8192, 8, 1024], P('ep', None, 'dp'), may hold values from -6 to 6
Outputs:
- hidden: bfloat16 [8192, 8, 1024], P('ep', None, 'dp')
- input_grad: bfloat16 [8192, 4096], P('ep', 'dp')
- grad_gate: bfloat16 [64, 4096, 1024], P('ep', 'dp')
- grad_up: bfloat16 [64, 4096, 1024], P('ep', 'dp')
Inputs may be any that keep to these rules, and one draw needn't show every extreme that they name: `routing`: the 8 experts of a token are different. In each aligned block of 128 rows (the rows of one index of ep) no expert is named by more than 8 rows, a bound that some block reaches.
All inputs are finite; a program needn't handle non-finite values.
Results may differ from a plain program's by a relative error of at most 0.025.
Values may be sent and summed in bfloat16 or wider, within the bound.
A program may use at most 64 MiB of HBM per device.

v0:
```python
import jax
import jax.numpy as jnp
from jax import lax
from jax.sharding import PartitionSpec as P


def swiglu_forward(preact, part_width):
    gate_pre = preact[:, :part_width]
    up_pre = preact[:, part_width:]
    return (gate_pre * jax.nn.sigmoid(gate_pre) * up_pre).astype(jnp.bfloat16)


def pair_grads(preact, upstream, part_width):
    row_count = preact.shape[0]
    block_count = preact.shape[1] // (2 * part_width)
    split_pre = preact.reshape(row_count, block_count, 2, part_width)
    gate_pre = split_pre[:, :, 0]
    up_pre = split_pre[:, :, 1]
    sigmoid_gate = jax.nn.sigmoid(gate_pre)
    upstream_f = upstream.reshape(row_count, block_count, part_width).astype(jnp.float32)
    d_gate = (upstream_f * up_pre * sigmoid_gate * (1.0 + gate_pre * (1.0 - sigmoid_gate))).astype(
        jnp.bfloat16
    )
    d_up = (upstream_f * gate_pre * sigmoid_gate).astype(jnp.bfloat16)
    return jnp.stack([d_gate, d_up], axis=2).reshape(row_count, block_count * 2 * part_width)


def local(tokens, routing, w_gate, w_up, cotangent):
    tok_rows, top_count = routing.shape
    feature_share = tokens.shape[1]
    hidden_width = w_gate.shape[2]
    experts = lax.axis_size("ep")
    groups = lax.axis_size("dp")
    part_width = hidden_width // groups
    capacity = 2 * tok_rows * top_count // (4 * experts)
    all_rows = experts * capacity
    contract_rows = (((0,), (0,)), ((), ()))
    contract_cols = (((1,), (1,)), ((), ()))
    chosen = routing.reshape(-1)
    onehot = (chosen[:, None] == jnp.arange(experts, dtype=jnp.int32)[None, :]).astype(jnp.int32)
    slot_index = jnp.sum((jnp.cumsum(onehot, axis=0) - onehot) * onehot, axis=1)
    position = jnp.where(chosen < experts, chosen * capacity + slot_index, -1)
    selector = (position[None, :] == jnp.arange(all_rows, dtype=jnp.int32)[:, None]).astype(
        jnp.bfloat16
    )
    token_select = selector.reshape(all_rows, tok_rows, top_count).sum(axis=2)
    outgoing = jnp.dot(token_select, tokens, preferred_element_type=jnp.float32).astype(
        jnp.bfloat16
    )
    arrived = lax.all_to_all(
        outgoing.reshape(experts, capacity, feature_share),
        "ep",
        split_axis=0,
        concat_axis=0,
        tiled=True,
    )
    rows_all = arrived.reshape(all_rows, feature_share)
    weights = jnp.concatenate(
        [
            w_gate[0].reshape(feature_share, groups, part_width),
            w_up[0].reshape(feature_share, groups, part_width),
        ],
        axis=2,
    )
    weights = weights.reshape(feature_share, 2 * hidden_width)
    term = jnp.dot(rows_all, weights, preferred_element_type=jnp.float32)
    pre_own = lax.psum_scatter(
        term.astype(jnp.bfloat16), "dp", scatter_dimension=1, tiled=True
    ).astype(jnp.float32)
    hidden_own = swiglu_forward(pre_own, part_width)
    returned_hidden = lax.all_to_all(
        hidden_own.reshape(experts, capacity, part_width),
        "ep",
        split_axis=0,
        concat_axis=0,
        tiled=True,
    )
    returned_hidden = returned_hidden.reshape(all_rows, part_width)
    hidden_slots = lax.dot_general(
        selector, returned_hidden, contract_rows, preferred_element_type=jnp.float32
    ).astype(jnp.bfloat16)
    hidden_slots = hidden_slots.reshape(tok_rows, top_count, part_width)
    flat_cot = cotangent.reshape(tok_rows * top_count, part_width)
    sent_cot = jnp.dot(selector, flat_cot, preferred_element_type=jnp.float32).astype(jnp.bfloat16)
    arrived_cot = lax.all_to_all(
        sent_cot.reshape(experts, capacity, part_width),
        "ep",
        split_axis=0,
        concat_axis=0,
        tiled=True,
    )
    arrived_cot = arrived_cot.reshape(all_rows, part_width)
    grads_own = pair_grads(pre_own, arrived_cot, part_width)
    rows_grad = lax.all_gather(grads_own, "dp", axis=1, tiled=True)
    block = lax.dot_general(rows_all, rows_grad, contract_rows, preferred_element_type=jnp.float32)
    grad_sum = block
    input_part = lax.dot_general(
        rows_grad, weights, contract_cols, preferred_element_type=jnp.float32
    )
    grad_sum, input_part = (grad_sum, input_part)
    dx_parts = input_part.astype(jnp.bfloat16).reshape(experts, capacity, feature_share)
    returned_dx = lax.all_to_all(dx_parts, "ep", split_axis=0, concat_axis=0, tiled=True)
    returned_dx = returned_dx.reshape(all_rows, feature_share)
    input_grad = lax.dot_general(
        token_select, returned_dx, contract_rows, preferred_element_type=jnp.float32
    ).astype(jnp.bfloat16)
    grad_bf = grad_sum.astype(jnp.bfloat16).reshape(feature_share, groups, 2, part_width)
    grad_gate = grad_bf[:, :, 0].reshape(feature_share, hidden_width)[None]
    grad_up = grad_bf[:, :, 1].reshape(feature_share, hidden_width)[None]
    return (hidden_slots, input_grad, grad_gate, grad_up)


def solution(mesh):
    in_specs = (
        P("ep", "dp"),
        P("ep", None),
        P("ep", "dp", None),
        P("ep", "dp", None),
        P("ep", None, "dp"),
    )
    out_specs = (P("ep", None, "dp"), P("ep", "dp"), P("ep", "dp", None), P("ep", "dp", None))
    return jax.shard_map(local, mesh=mesh, in_specs=in_specs, out_specs=out_specs, check_vma=False)
```

profile of v0, /device:TPU:1, one launch (start us, length us, event | category | flops | bytes accessed | tf_op | source)
XLA Modules:
  0.0 183.6 jit_solution(4741668254378461860)
XLA Ops:
  7.2 0.0 copy-start
  7.2 0.0 copy-start.8
  7.2 0.0 copy-start.7
  7.2 0.8 copy.44
  8.0 0.1 reshape.130
  8.1 0.1 eq.46
  8.3 0.0 copy-start.3
  8.3 18.0 %reduce-window.6 = s32[64,8,128]{2,1,0:T(8,128)S(1)} reduce-window(s32[64,8,128]{2,1,0:T(8,128)S(1)} %fusion.25, s32[]{:T(128)} %constant.4.clone.1), window={size=1x1x128 pad=0_0x0_0x127_0}, to_apply=%region_0.0 | reduce-window | flops 8323072 | bytes 524292 | tf_op jit(solution)/shard_map/reduce-window
  26.3 0.1 slice.32
  26.4 0.1 copy.46
  26.6 0.1 copy.47
  26.7 0.1 broadcast_add_fusion
  26.8 0.1 fusion.22
  26.9 0.0 copy-start.4
  26.9 0.1 reduce_sum.24
  27.1 0.0 copy-done.8
  27.1 0.9 fusion.9
  28.0 0.0 copy-done.7
  28.0 1.1 fusion.3
  29.1 17.1 %all-to-all-start = ((bf16[64,8,512]{2,1,0:T(8,128)(2,1)}), bf16[64,8,512]{2,1,0:T(8,128)(2,1)S(1)}, u32[]{:S(2)}, u32[]{:S(2)}) async-start(bf16[64,8,512]{2,1,0:T(8,128)(2,1)} %fusion.3), calls=%async_computation | async-start | bytes 1048576 | tf_op jit(solution)/shard_map/all_to_all | solution.py:50
  46.2 0.0 reduce-scatter.2.cloned.1.call-start
  46.2 0.0 copy-done.3
  46.3 0.3 copy.62
  46.5 0.0 copy-done.4
  46.5 0.3 copy.63
  46.8 0.2 pad_maximum_fusion
  47.1 0.7 copy.64
  47.7 14.8 %all-to-all-done = bf16[64,8,512]{2,1,0:T(8,128)(2,1)S(1)} async-done(((bf16[64,8,512]{2,1,0:T(8,128)(2,1)}), bf16[64,8,512]{2,1,0:T(8,128)(2,1)S(1)}, u32[]{:S(2)}, u32[]{:S(2)}) %all-to-all-start) | async-done | bytes 524320 | tf_op jit(solution)/shard_map/all_to_all | solution.py:50
  62.6 0.0 copy-start.5
  62.6 2.6 %convolution_convert_fusion.1 = bf16[512,2048]{1,0:T(8,128)(2,1)} fusion(bf16[512,2048]{1,0:T(8,128)(2,1)S(1)} %bitcast.70, bf16[64,8,512]{2,1,0:T(8,128)(2,1)S(1)} %all-to-all-done), kind=kOutput, calls=%fused_computation.1 | convolution fusion | flops 1074790400 | bytes 4718592 | tf_op jit(solution)/shard_map/dot_general | solution.py:66
  65.2 0.0 copy-done.5
  65.2 0.0 reduce-scatter.2.cloned.1.call-update
  65.2 0.0 copy-done
  65.2 1.1 fusion.8
  66.3 8.1 %all-to-all-start.2 = ((bf16[64,8,128]{2,1,0:T(8,128)(2,1)}), bf16[64,8,128]{2,1,0:T(8,128)(2,1)}, u32[]{:S(2)}, u32[]{:S(2)}) async-start(bf16[64,8,128]{2,1,0:T(8,128)(2,1)} %fusion.8), calls=%async_computation.3 | async-start | bytes 262144 | tf_op jit(solution)/shard_map/all_to_all | solution.py:85
  74.4 0.0 all-gather.2.cloned.1.call-start
  74.4 25.1 %reduce-scatter.2.cloned.1.call-done = bf16[512,256]{1,0:T(8,128)(2,1)} async-done(((bf16[512,2048]{1,0:T(8,128)(2,1)}), bf16[512,256]{1,0:T(8,128)(2,1)}) %reduce-scatter.2.cloned.1.call-update) | async-done | bytes 262160 | tf_op jit(solution)/shard_map/reduce_scatter | solution.py:67
  99.6 1.1 copy.49
  100.7 0.0 copy-start.2
  100.7 0.7 fusion.29
  101.4 1.1 copy.57
  102.5 0.1 copy.58
  102.6 0.0 all-to-all-done.2
  102.6 1.0 fusion.17
  103.7 0.9 copy.52
  104.6 0.0 all-gather.2.cloned.1.call-update
  104.6 0.0 copy-done.2
  104.7 0.1 fusion.27
  104.7 23.1 %all_to_all.20 = bf16[64,8,128]{2,1,0:T(8,128)(2,1)S(1)} all-to-all(bf16[64,8,128]{2,1,0:T(8,128)(2,1)S(1)} %fusion.27), channel_id=1, replica_groups=mesh['ep'=64,'dp'=8] {'ep'}, dimensions={0} | all-to-all | bytes 262144 | tf_op jit(solution)/shard_map/all_to_all | solution.py:71
  127.8 1.4 fusion.6
  129.3 6.8 %all-gather.2.cloned.1.call-done = bf16[512,2048]{0,1:T(8,128)(2,1)} async-done(((bf16[512,256]{0,1:T(8,128)(2,1)}), bf16[512,2048]{0,1:T(8,128)(2,1)}) %all-gather.2.cloned.1.call-update) | async-done | bytes 2097168 | tf_op jit(solution)/shard_map/all_gather | solution.py:94
  136.0 3.7 %fusion.4 = bf16[64,8,512]{2,1,0:T(8,128)(2,1)} fusion(bf16[512,2048]{0,1:T(8,128)(2,1)} %all-gather.2.cloned.1.call-done, bf16[512,2048]{1,0:T(8,128)(2,1)S(1)} %bitcast.71), kind=kOutput, calls=%fused_computation.11 | convolution fusion | flops 1074003968 | bytes 4718592 | tf_op jit(solution)/shard_map/dot_general | solution.py:97
  139.7 13.5 %all-to-all-start.3 = ((bf16[64,8,512]{2,1,0:T(8,128)(2,1)}), bf16[64,8,512]{2,1,0:T(8,128)(2,1)}, u32[]{:S(2)}, u32[]{:S(2)}) async-start(bf16[64,8,512]{2,1,0:T(8,128)(2,1)} %fusion.4), calls=%async_computation.4 | async-start | bytes 1048576 | tf_op jit(solution)/shard_map/all_to_all | solution.py:102
  153.2 0.0 copy-done.6
  153.2 4.2 %convolution_convert_fusion = bf16[512,2048]{1,0:T(8,128)(2,1)} fusion(bf16[512,2048]{0,1:T(8,128)(2,1)} %all-gather.2.cloned.1.call-done, bf16[64,8,512]{2,1,0:T(8,128)(2,1)S(1)} %copy-done.6), kind=kOutput, calls=%fused_computation | convolution fusion | flops 1074790400 | bytes 4718592 | tf_op jit(solution)/shard_map/dot_general | solution.py:95
  157.4 3.2 %reshape.144 = bf16[512,8,2,128]{3,2,1,0:T(2,128)(2,1)S(1)} reshape(bf16[512,2048]{1,0:T(8,128)(2,1)} %convolution_convert_fusion) | data formatting | bytes 4194304 | tf_op jit(solution)/shard_map/reshape | solution.py:107
  160.7 4.2 %fusion.28 = (bf16[512,8,1,128]{3,2,1,0:T(2,128)(2,1)}, bf16[512,8,1,128]{3,2,1,0:T(2,128)(2,1)}) fusion(bf16[512,8,2,128]{3,2,1,0:T(2,128)(2,1)S(1)} %reshape.144), kind=kLoop, calls=%fused_computation.47 | loop fusion | bytes 4194304 | tf_op jit(solution)/shard_map/slice | solution.py:109
  164.8 4.7 %copy.60 = bf16[512,8,1,128]{0,3,1,2:T(8,128)(2,1)S(1)} copy(bf16[512,8,1,128]{3,2,1,0:T(2,128)(2,1)} %get-tuple-element.20) | data formatting | bytes 2097152
  169.5 1.3 copy.56
  170.9 0.0 copy-done.1
  170.9 2.6 %copy.59 = bf16[512,8,1,128]{0,3,1,2:T(8,128)(2,1)S(1)} copy(bf16[512,8,1,128]{3,2,1,0:T(2,128)(2,1)S(1)} %copy-done.1) | data formatting | bytes 2097152
  173.5 1.3 copy.55
  174.8 0.0 all-to-all-done.3
  174.8 2.0 %convolution_convert_fusion.4 = bf16[128,512]{1,0:T(8,128)(2,1)} fusion(bf16[512,128]{1,0:T(8,128)(2,1)S(1)} %fusion.9, bf16[64,8,512]{2,1,0:T(8,128)(2,1)} %all-to-all-done.3), kind=kOutput, calls=%fused_computation.15 | convolution fusion | flops 67174400 | bytes 786432 | tf_op jit(solution)/shard_map/dot_general | solution.py:104
  (10 shorter events, 0.2 us)
Async XLA Ops:
  7.2 58.0 %copy-start = (bf16[128,8,128]{2,1,0:T(8,128)(2,1)S(1)}, bf16[128,8,128]{2,1,0:T(8,128)(2,1)}, u32[]{:S(2)}) copy-start(bf16[128,8,128]{2,1,0:T(8,128)(2,1)} %param.9) | copy-start | bytes 786436
  7.2 19.9 %copy-start.8 = (s32[128,8]{0,1:T(8,128)S(1)}, s32[128,8]{0,1:T(8,128)}, u32[]{:S(2)}) copy-start(s32[128,8]{0,1:T(8,128)} %param.6) | copy-start | bytes 12292
  7.2 20.8 %copy-start.7 = (bf16[128,512]{1,0:T(8,128)(2,1)S(1)}, bf16[128,512]{1,0:T(8,128)(2,1)}, u32[]{:S(2)}) copy-start(bf16[128,512]{1,0:T(8,128)(2,1)} %param.5) | copy-start | bytes 393220
  8.3 38.0 %copy-start.3 = (bf16[1,512,1024]{2,1,0:T(8,128)(2,1)S(1)}, bf16[1,512,1024]{2,1,0:T(8,128)(2,1)}, u32[]{:S(2)}) copy-start(bf16[1,512,1024]{2,1,0:T(8,128)(2,1)} %param.7) | copy-start | bytes 3145732
  26.9 19.6 %copy-start.4 = (bf16[1,512,1024]{2,1,0:T(8,128)(2,1)S(1)}, bf16[1,512,1024]{2,1,0:T(8,128)(2,1)}, u32[]{:S(2)}) copy-start(bf16[1,512,1024]{2,1,0:T(8,128)(2,1)} %param.8) | copy-start | bytes 3145732
  29.1 33.5 %all-to-all-start = ((bf16[64,8,512]{2,1,0:T(8,128)(2,1)}), bf16[64,8,512]{2,1,0:T(8,128)(2,1)S(1)}, u32[]{:S(2)}, u32[]{:S(2)}) async-start(bf16[64,8,512]{2,1,0:T(8,128)(2,1)} %fusion.3), calls=%async_computation | async-start | bytes 1048576 | tf_op jit(solution)/shard_map/all_to_all | solution.py:50
  46.2 53.4 %reduce-scatter.2.cloned.1.call-start = ((), (), s32[]{:S(2)}) async-start(), calls=%async_computation.5 | async-start | bytes 2359296 | tf_op jit(solution)/shard_map/reduce_scatter | solution.py:67
  62.6 2.6 %copy-start.5 = (bf16[64,8,512]{2,1,0:T(8,128)(2,1)}, bf16[64,8,512]{2,1,0:T(8,128)(2,1)S(1)}, u32[]{:S(2)}) copy-start(bf16[64,8,512]{2,1,0:T(8,128)(2,1)S(1)} %all-to-all-done) | copy-start | bytes 1572868
  66.3 36.3 %all-to-all-start.2 = ((bf16[64,8,128]{2,1,0:T(8,128)(2,1)}), bf16[64,8,128]{2,1,0:T(8,128)(2,1)}, u32[]{:S(2)}, u32[]{:S(2)}) async-start(bf16[64,8,128]{2,1,0:T(8,128)(2,1)} %fusion.8), calls=%async_computation.3 | async-start | bytes 262144 | tf_op jit(solution)/shard_map/all_to_all | solution.py:85
  74.4 61.7 %all-gather.2.cloned.1.call-start = ((), (), s32[]{:S(2)}) async-start(), calls=%async_computation.6 | async-start | bytes 2359296 | tf_op jit(solution)/shard_map/all_gather | solution.py:94
  100.7 3.9 %copy-start.2 = (bf16[512,256]{1,0:T(8,128)(2,1)S(1)}, bf16[512,256]{1,0:T(8,128)(2,1)}, u32[]{:S(2)}) copy-start(bf16[512,256]{1,0:T(8,128)(2,1)} %reduce-scatter.2.cloned.1.call-done) | copy-start | bytes 786436
  129.3 23.9 %copy-start.6 = (bf16[64,8,512]{2,1,0:T(8,128)(2,1)S(1)}, bf16[64,8,512]{2,1,0:T(8,128)(2,1)}, u32[]{:S(2)}) copy-start(bf16[64,8,512]{2,1,0:T(8,128)(2,1)} %copy-done.5) | copy-start | bytes 1572868
  139.7 35.0 %all-to-all-start.3 = ((bf16[64,8,512]{2,1,0:T(8,128)(2,1)}), bf16[64,8,512]{2,1,0:T(8,128)(2,1)}, u32[]{:S(2)}, u32[]{:S(2)}) async-start(bf16[64,8,512]{2,1,0:T(8,128)(2,1)} %fusion.4), calls=%async_computation.4 | async-start | bytes 1048576 | tf_op jit(solution)/shard_map/all_to_all | solution.py:102
  164.8 6.0 %copy-start.1 = (bf16[512,8,1,128]{3,2,1,0:T(2,128)(2,1)S(1)}, bf16[512,8,1,128]{3,2,1,0:T(2,128)(2,1)}, u32[]{:S(2)}) copy-start(bf16[512,8,1,128]{3,2,1,0:T(2,128)(2,1)} %get-tuple-element.21) | copy-start | bytes 3145732
Sparse Core Ops, SparseCore 0:
  65.3 34.2 reduce-scatter.1
  104.7 31.2 all-gather.1
where the time goes:
time: 184 us
  waiting for transfers between devices  46.8 us (25%)
  starting transfers between devices  38.7 us (21%)
  local copies, waits for them, and re-layouts  24 us (13%)
  blocking collectives  23.1 us (13%)
  other arithmetic  20.6 us (11%)
  matrix products  16.1 us (9%)
  between operations  14.3 us (8%)
    reduce_scatter x1, waiting for transfers between devices, local(): lax.psum_scatter(term.astype(jnp.bfloat16), 'dp', scatter_dimension=1, ti...  25.1 us
    all_to_all x1, blocking collectives, local(): lax.all_to_all(hidden_own.reshape(experts, capacity, part_width), 'ep', s...  23.1 us
    another operation x3, other arithmetic  18.2 us
    all_to_all x1, starting transfers between devices, local(): lax.all_to_all(outgoing.reshape(experts, capacity, feature_share), 'ep',...  17.1 us
    all_to_all x1, waiting for transfers between devices, local(): lax.all_to_all(outgoing.reshape(experts, capacity, feature_share), 'ep',...  14.8 us
    all_to_all x1, starting transfers between devices, local(): lax.all_to_all(dx_parts, 'ep', split_axis=0, concat_axis=0, tiled=True)  13.5 us
    unnamed x28, local copies, waits for them, and re-layouts  13.2 us
    all_to_all x1, starting transfers between devices, local(): lax.all_to_all(sent_cot.reshape(experts, capacity, part_width), 'ep', spl...  8.05 us
  transfers between devices with their start and end apart: 5, of which 3 were waited for; matrix products, arithmetic and copies ran while one was open for 16% of the time, Pallas kernels for 0%

commit v1 on v0

v1 whole, which is shorter than its diff:
```python
import functools
import math

import jax
import jax.numpy as jnp
from jax import lax
from jax.experimental import pallas as pl
from jax.experimental.pallas import tpu as pltpu
from jax.sharding import PartitionSpec as P

MESH = pl.DeviceIdType.MESH
BF16 = jnp.bfloat16
F32 = jnp.float32
CAP = 8
CHUNKS = 4


def dot(a, b, dims=(((1,), (0,)), ((), ()))):
    return lax.dot_general(a, b, dims, preferred_element_type=F32)


def fold(i, n):
    c, p = i // 2, i % 2
    moved = (c + n - 1) // n
    return (1 - p) * c + p * (n - c) - p * (n // 2) * (1 - moved)


def fold_vector(i, n):
    c, p = i >> 1, i & 1
    return jnp.where(p == 0, c, jnp.where(c == 0, n // 2, n - c))


def kernel(
    ny, nz, nx,
    tok_hbm, rout_hbm, wg_hbm, wu_hbm, cot_hbm,
    hid_out, dx_out, gg_out, gu_out,
    tok, rout, cot, w, send_d, recv_d, sel_t, sel_p, sel_pt,
    own_a, send_a, recv_a, own_b, send_b, recv_b, d_pair, send_r, recv_r, hid, grad, hid_v, dx_v,
    in_sem, w_sem, sd_sem, rd_sem, sa_sem, ra_sem, sb_sem, rb_sem, sg_sem, rg_sem, sh_sem, rh_sem,
    sr_sem, rr_sem, out_sem,
):
    experts = ny * nz
    tokens, features = tok.shape
    top = rout.shape[0]
    pairs = cot.shape[0]
    part = cot.shape[1]
    group = experts // CHUNKS
    rows = group * CAP
    me, mine = lax.axis_index("ep"), lax.axis_index("dp")
    y, z = me // nz, me % nz
    x, core = mine // 2, mine % 2
    partner = x * 2 + 1 - core

    def along_x(step):
        return (x + step) % nx * 2 + core

    def block_of(k):
        return along_x(k) if k < nx else (x + k - nx) % nx * 2 + 1 - core

    def to_expert(o):
        dy, dz = fold(o // nz, ny), fold(o % nz, nz)
        return (y + dy) % ny * nz + (z + dz) % nz

    def to_source(o):
        dy, dz = fold(o // nz, ny), fold(o % nz, nz)
        return (y + ny - dy) % ny * nz + (z + nz - dz) % nz

    small = [
        pltpu.make_async_copy(rout_hbm, rout, in_sem.at[0]),
        pltpu.make_async_copy(tok_hbm, tok, in_sem.at[1]),
        pltpu.make_async_copy(cot_hbm, cot, in_sem.at[2]),
    ]
    for copy in small:
        copy.start()
    w_copies = []
    for k in range(2 * nx):
        at = pl.ds(pl.multiple_of(block_of(k) * part, part), part)
        for n, source in enumerate((wg_hbm, wu_hbm)):
            copy = pltpu.make_async_copy(source.at[0, :, at], w.at[k, :, pl.ds(n * part, part)], w_sem.at[k, n])
            copy.start()
            w_copies.append(copy)

    barrier = pltpu.get_barrier_semaphore()

    @pl.loop(1, experts)
    def _(o):
        pl.semaphore_signal(barrier, inc=1, device_id=(to_expert(o), mine), device_id_type=MESH)

    for step in range(1, nx):
        pl.semaphore_signal(barrier, inc=1, device_id=(me, along_x(step)), device_id_type=MESH)
    pl.semaphore_signal(barrier, inc=1, device_id=(me, partner), device_id_type=MESH)

    small[0].wait()
    routes = rout[...]
    before = (
        lax.broadcasted_iota(jnp.int32, (tokens, tokens), 0) < lax.broadcasted_iota(jnp.int32, (tokens, tokens), 1)
    ).astype(F32).astype(BF16)
    spread = (
        lax.broadcasted_iota(jnp.int32, (tokens, pairs), 1) // top == lax.broadcasted_iota(jnp.int32, (tokens, pairs), 0)
    ).astype(F32).astype(BF16)
    named = dot(routes.astype(F32).astype(BF16), spread)
    place = lax.broadcasted_iota(jnp.int32, (top, pairs), 1) % top == lax.broadcasted_iota(jnp.int32, (top, pairs), 0)
    chosen = jnp.sum(jnp.where(place, named, 0.0), axis=0, keepdims=True)
    small[1].wait()
    small[2].wait()
    for c in range(CHUNKS):
        row = lax.broadcasted_iota(jnp.int32, (rows, tokens), 0)
        o = row // CAP + c * group
        dy, dz = fold_vector(o // nz, ny), fold_vector(o % nz, nz)
        expert = ((y + dy) & (ny - 1)) * nz + ((z + dz) & (nz - 1))
        slot = (row % CAP).astype(F32)
        hit = routes[0:1, :] == expert
        for k in range(1, top):
            hit = hit | (routes[k : k + 1, :] == expert)
        hit = hit.astype(F32)
        earlier = dot(hit.astype(BF16), before)
        sel = jnp.where(earlier == slot, hit, 0.0)
        picked = sel.astype(BF16)
        out_tok = dot(picked, tok[...]).astype(BF16)
        expanded = dot(picked, spread)
        expert_p = expert.astype(F32)[:, 0:1]
        sel_pair = jnp.where((chosen == expert_p), expanded, 0.0).astype(BF16)
        out_cot = dot(sel_pair, cot[...]).astype(BF16)
        outgoing = jnp.concatenate([out_tok, out_cot], axis=1).reshape(group, CAP, features + part)
        send_d[c * group : (c + 1) * group] = outgoing
        if c == 0:
            recv_d[0:1] = outgoing[0:1]
            pl.semaphore_wait(barrier, experts + nx - 1)

        @pl.loop(max(1, c * group), (c + 1) * group)
        def _(o):
            pltpu.make_async_remote_copy(
                src_ref=send_d.at[o],
                dst_ref=recv_d.at[o],
                send_sem=sd_sem.at[c],
                recv_sem=rd_sem.at[c],
                device_id=(to_expert(o), mine),
                device_id_type=MESH,
            ).start()

        sel_t[c] = sel.T.astype(BF16)
        sel_p[c] = sel_pair

    for c in range(CHUNKS):
        sel_pt[c] = sel_p[c].astype(F32).T.astype(BF16)
    for copy in w_copies:
        copy.wait()

    def wait_for(ref, sem):
        pltpu.make_async_copy(ref, ref, sem).wait()

    def remote(source, target, send_sem, recv_sem, device):
        pltpu.make_async_remote_copy(
            src_ref=source,
            dst_ref=target,
            send_sem=send_sem,
            recv_sem=recv_sem,
            device_id=(me, device),
            device_id_type=MESH,
        ).start()

    def span(c):
        first = max(1, c * group)
        return pl.ds(first, (c + 1) * group - first)

    def arrived(c):
        return recv_d[c * group : (c + 1) * group].reshape(rows, features + part)

    def project(c):
        wait_for(recv_d.at[span(c)], rd_sem.at[c])
        held = arrived(c)[:, :features]
        for k in range(nx):
            send_a[c, k] = dot(held, w[nx + k]).astype(BF16)
        remote(send_a.at[c], recv_a.at[c], sa_sem.at[c], ra_sem.at[c], partner)
        for k in range(nx):
            own_a[c, k] = dot(held, w[k])

    def add_partner(c):
        wait_for(recv_a.at[c], ra_sem.at[c])
        for k in range(1, nx):
            send_b[c, k - 1] = (own_a[c, k] + recv_a[c, k].astype(F32)).astype(BF16)
            remote(send_b.at[c, k - 1], recv_b.at[c, k - 1], sb_sem.at[c, k - 1], rb_sem.at[c, k - 1], along_x(k))
        own_b[c] = own_a[c, 0] + recv_a[c, 0].astype(F32)

    def activate(c):
        for k in range(1, nx):
            wait_for(recv_b.at[c, k - 1], rb_sem.at[c, k - 1])
        pre = own_b[c]
        for k in range(1, nx):
            pre = pre + recv_b[c, k - 1].astype(F32)
        gate_pre, up_pre = pre[:, :part], pre[:, part:]
        upstream = arrived(c)[:, features:].astype(F32)
        s = jax.nn.sigmoid(gate_pre)
        d_gate = upstream * up_pre * s * (1.0 + gate_pre * (1.0 - s))
        d_up = upstream * gate_pre * s
        d_pair[c, 0] = jnp.concatenate([d_gate, d_up], axis=1).astype(BF16)
        for k in range(1, nx):
            remote(d_pair.at[c, 0], d_pair.at[c, nx - k], sg_sem.at[c, k - 1], rg_sem.at[c, nx - k], along_x(k))
        remote(d_pair.at[c, 0], d_pair.at[c, nx], sh_sem.at[c, 0], rh_sem.at[c, 0], partner)
        hid[c] = (gate_pre * s * up_pre).astype(BF16)

    def forward(c):
        for k in (*range(1, nx, 2), *range(2, nx, 2)):
            wait_for(d_pair.at[c, k], rg_sem.at[c, k])
            remote(d_pair.at[c, k], d_pair.at[c, nx + k], sh_sem.at[c, k], rh_sem.at[c, k], partner)

    def give_back(c):
        for k in range(nx):
            wait_for(d_pair.at[c, nx + k], rh_sem.at[c, k])
        total = dot(d_pair[c, 0], w[0], (((1,), (1,)), ((), ())))
        for k in range(1, 2 * nx):
            total = total + dot(d_pair[c, k], w[k], (((1,), (1,)), ((), ())))
        back = jnp.concatenate([total.astype(BF16), hid[c]], axis=1).reshape(group, CAP, features + part)
        send_r[c * group : (c + 1) * group] = back
        if c == 0:
            recv_r[0:1] = back[0:1]

        @pl.loop(max(1, c * group), (c + 1) * group)
        def _(o):
            pltpu.make_async_remote_copy(
                src_ref=send_r.at[o],
                dst_ref=recv_r.at[o],
                send_sem=sr_sem.at[c],
                recv_sem=rr_sem.at[c],
                device_id=(to_source(o), mine),
                device_id_type=MESH,
            ).start()

    stages = (project, add_partner, activate, forward, give_back)
    for step in range(CHUNKS + len(stages) - 1):
        for late, stage in enumerate(stages):
            if 0 <= step - late < CHUNKS:
                stage(step - late)

    held = jnp.concatenate([arrived(c)[:, :features] for c in range(CHUNKS)], axis=0)
    out_copies = []
    for k in range(2 * nx):
        both = d_pair[:, k].reshape(CHUNKS * rows, 2 * part)
        grad[k] = dot(held, both, (((0,), (0,)), ((), ()))).astype(BF16)
        at = pl.ds(pl.multiple_of(block_of(k) * part, part), part)
        for n, target in enumerate((gg_out, gu_out)):
            copy = pltpu.make_async_copy(grad.at[k, :, pl.ds(n * part, part)], target.at[0, :, at], w_sem.at[k, n])
            copy.start()
            out_copies.append(copy)

    total = jnp.zeros((tokens, features), F32)
    hidden = jnp.zeros((pairs, part), F32)
    for c in range(CHUNKS):
        wait_for(recv_r.at[span(c)], rr_sem.at[c])
        back = recv_r[c * group : (c + 1) * group].reshape(rows, features + part)
        total = total + dot(sel_t[c], back[:, :features])
        hidden = hidden + dot(sel_pt[c], back[:, features:])
    dx_v[...] = total.astype(BF16)
    copy = pltpu.make_async_copy(dx_v, dx_out, out_sem.at[0])
    copy.start()
    out_copies.append(copy)
    hid_v[...] = hidden.astype(BF16)
    copy = pltpu.make_async_copy(hid_v, hid_out, out_sem.at[1])
    copy.start()
    out_copies.append(copy)

    for c in range(CHUNKS):
        wait_for(send_d.at[span(c)], sd_sem.at[c])
        wait_for(send_a.at[c], sa_sem.at[c])
        for k in range(1, nx):
            wait_for(send_b.at[c, k - 1], sb_sem.at[c, k - 1])
            wait_for(d_pair.at[c, 0], sg_sem.at[c, k - 1])
        for k in range(nx):
            wait_for(d_pair.at[c, k], sh_sem.at[c, k])
        wait_for(send_r.at[span(c)], sr_sem.at[c])
    for copy in out_copies:
        copy.wait()


def local(ny, nz, nx, tokens, routing, w_gate, w_up, cotangent):
    tok_rows, top = routing.shape
    features = tokens.shape[1]
    part = cotangent.shape[2]
    hidden_width = w_gate.shape[2]
    experts = ny * nz
    pairs = tok_rows * top
    rows = experts // CHUNKS * CAP
    flat = cotangent.reshape(pairs, part)
    any_ref = pl.BlockSpec(memory_space=pl.ANY)
    wide = features + part
    dma = pltpu.SemaphoreType.DMA
    hidden, dx, gg, gu = pl.pallas_call(
        functools.partial(kernel, ny, nz, nx),
        out_shape=(
            jax.ShapeDtypeStruct((pairs, part), BF16),
            jax.ShapeDtypeStruct((tok_rows, features), BF16),
            jax.ShapeDtypeStruct((1, features, hidden_width), BF16),
            jax.ShapeDtypeStruct((1, features, hidden_width), BF16),
        ),
        in_specs=[any_ref] * 5,
        out_specs=(any_ref,) * 4,
        scratch_shapes=[
            pltpu.VMEM((tok_rows, features), BF16),
            pltpu.VMEM((top, tok_rows), jnp.int32),
            pltpu.VMEM((pairs, part), BF16),
            pltpu.VMEM((2 * nx, features, 2 * part), BF16),
            pltpu.VMEM((experts, CAP, wide), BF16),
            pltpu.VMEM((experts, CAP, wide), BF16),
            pltpu.VMEM((CHUNKS, tok_rows, rows), BF16),
            pltpu.VMEM((CHUNKS, rows, pairs), BF16),
            pltpu.VMEM((CHUNKS, pairs, rows), BF16),
            pltpu.VMEM((CHUNKS, nx, rows, 2 * part), F32),
            pltpu.VMEM((CHUNKS, nx, rows, 2 * part), BF16),
            pltpu.VMEM((CHUNKS, nx, rows, 2 * part), BF16),
            pltpu.VMEM((CHUNKS, rows, 2 * part), F32),
            pltpu.VMEM((CHUNKS, nx - 1, rows, 2 * part), BF16),
            pltpu.VMEM((CHUNKS, nx - 1, rows, 2 * part), BF16),
            pltpu.VMEM((CHUNKS, 2 * nx, rows, 2 * part), BF16),
            pltpu.VMEM((experts, CAP, wide), BF16),
            pltpu.VMEM((experts, CAP, wide), BF16),
            pltpu.VMEM((CHUNKS, rows, part), BF16),
            pltpu.VMEM((2 * nx, features, 2 * part), BF16),
            pltpu.VMEM((pairs, part), BF16),
            pltpu.VMEM((tok_rows, features), BF16),
            dma((3,)),
            dma((2 * nx, 2)),
            dma((CHUNKS,)),
            dma((CHUNKS,)),
            dma((CHUNKS,)),
            dma((CHUNKS,)),
            dma((CHUNKS, nx - 1)),
            dma((CHUNKS, nx - 1)),
            dma((CHUNKS, nx - 1)),
            dma((CHUNKS, nx)),
            dma((CHUNKS, nx)),
            dma((CHUNKS, nx)),
            dma((CHUNKS,)),
            dma((CHUNKS,)),
            dma((2,)),
        ],
        compiler_params=pltpu.CompilerParams(
            collective_id=0, has_side_effects=True, vmem_limit_bytes=48 * 1024 * 1024
        ),
        name="experts",
    )(tokens, routing.T, w_gate, w_up, flat)
    return hidden.reshape(tok_rows, top, part), dx, gg, gu


def solution(mesh):
    experts, groups = mesh.shape["ep"], mesh.shape["dp"]
    ny = math.isqrt(experts)
    nz = experts // ny
    in_specs = (
        P("ep", "dp"),
        P("ep", None),
        P("ep", "dp", None),
        P("ep", "dp", None),
        P("ep", None, "dp"),
    )
    out_specs = (P("ep", None, "dp"), P("ep", "dp"), P("ep", "dp", None), P("ep", "dp", None))
    return jax.shard_map(
        functools.partial(local, ny, nz, groups // 2), mesh=mesh, in_specs=in_specs, out_specs=out_specs, check_vma=False
    )
```

time: 184 us -> 85.6 us (0.47)
  Pallas kernels: 0 us -> 76.4 us
  waiting for transfers between devices: 46.8 us -> 0 us
  starting transfers between devices: 38.7 us -> 0 us
  blocking collectives: 23.1 us -> 0 us
  other arithmetic: 20.6 us -> 0 us
  matrix products: 16.1 us -> 0 us
  local copies, waits for them, and re-layouts: 24 us -> 8.28 us
  between operations: 14.3 us -> 0.65 us
    pallas_call x0 -> x1, Pallas kernels: none -> 76.4 us  [local(): pl.pallas_call(functools.partial(kernel, ny, nz, nx), out_shape=(jax.Shap...]
    all_to_all x3 -> x0, starting transfers between devices: 38.6 us -> none  [the longest x1 17.1 us: local(): lax.all_to_all(outgoing.reshape(experts, capacity, feature_share), 'ep',...]
    reduce_scatter x1 -> x0, waiting for transfers between devices: 25.1 us -> none  [local(): lax.psum_scatter(term.astype(jnp.bfloat16), 'dp', scatter_dimension=1, ti...]
    all_to_all x1 -> x0, blocking collectives: 23.1 us -> none  [local(): lax.all_to_all(hidden_own.reshape(experts, capacity, part_width), 'ep', s...]
    another operation x4 -> x0, other arithmetic: 18.2 us -> none
    dot_general x7 -> x0, matrix products: 16.1 us -> none  [the longest x1 4.22 us: local(): lax.dot_general(rows_all, rows_grad, contract_rows, preferred_element_typ...]
    all_to_all x3 -> x0, waiting for transfers between devices: 14.8 us -> none  [the longest x1 14.8 us: local(): lax.all_to_all(outgoing.reshape(experts, capacity, feature_share), 'ep',...]
    all_gather x1 -> x0, waiting for transfers between devices: 6.78 us -> none  [local(): rows_grad = lax.all_gather(grads_own, 'dp', axis=1, tiled=True)]
  transfers between devices with their start and end apart: 5 -> 0, of which waited for: 3 -> 0; matrix products, arithmetic and copies ran while one was open for 16% -> 0% of each run, Pallas kernels for 0% -> 0%
where the time goes in v1:
time: 85.6 us; the launch traced here: 85.4 us
  Pallas kernels  76.4 us (89%)
  local copies, waits for them, and re-layouts  8.28 us (10%)
    pallas_call x1, Pallas kernels, local(): pl.pallas_call(functools.partial(kernel, ny, nz, nx), out_shape=(jax.Shap...  76.4 us
    unnamed x14, local copies, waits for them, and re-layouts  8.28 us

profile of v1, /device:TPU:1, one launch (start us, length us, event | category | flops | bytes accessed | tf_op | source)
XLA Modules:
  0.0 85.4 jit_solution(4420893008522591254)
XLA Ops:
  0.6 0.0 copy-start
  0.6 1.2 %copy-done = bf16[1,512,1024]{2,1,0:T(8,128)(2,1)S(1)} copy-done((bf16[1,512,1024]{2,1,0:T(8,128)(2,1)S(1)}, bf16[1,512,1024]{2,1,0:T(8,128)(2,1)}, u32[]{:S(2)}) %copy-start) | copy-done | bytes 1048600
  1.9 0.0 copy-start.1
  1.9 1.2 %copy-done.1 = bf16[1,512,1024]{2,1,0:T(8,128)(2,1)S(1)} copy-done((bf16[1,512,1024]{2,1,0:T(8,128)(2,1)S(1)}, bf16[1,512,1024]{2,1,0:T(8,128)(2,1)}, u32[]{:S(2)}) %copy-start.1) | copy-done | bytes 1048600
  3.1 0.0 copy-start.2
  3.1 0.9 %copy-done.2 = bf16[128,8,128]{2,1,0:T(8,128)(2,1)S(1)} copy-done((bf16[128,8,128]{2,1,0:T(8,128)(2,1)S(1)}, bf16[128,8,128]{2,1,0:T(8,128)(2,1)}, u32[]{:S(2)}) %copy-start.2) | copy-done | bytes 262168
  4.0 0.0 copy-start.3
  4.0 0.9 %copy-done.3 = bf16[128,512]{1,0:T(8,128)(2,1)S(1)} copy-done((bf16[128,512]{1,0:T(8,128)(2,1)S(1)}, bf16[128,512]{1,0:T(8,128)(2,1)}, u32[]{:S(2)}) %copy-start.3) | copy-done | bytes 131096
  4.9 0.0 copy-start.4
  4.9 0.7 copy-done.4
  5.6 76.4 %experts.1 = (bf16[1024,128]{1,0:T(8,128)(2,1)S(1)}, bf16[128,512]{1,0:T(8,128)(2,1)S(1)}, bf16[1,512,1024]{2,1,0:T(8,128)(2,1)S(1)}, bf16[1,512,1024]{2,1,0:T(8,128)(2,1)S(1)}) custom-call(bf16[128,512]{1,0:T(8,128)(2,1)S(1)} %copy-done.3, s32[8,128]{1,0:T(8,128)S(1)} %bitcast.5, bf16[1,512,1024]{2,1,0:T(8,128)(2,1)S(1)} %copy-done, ...), custom_call_target="tpu_custom_call" | custom-call | tf_op jit(solution)/shard_map/experts/pallas_call | solution.py:287
  82.1 0.7 copy.13
  82.8 0.7 copy.14
  83.4 1.0 %copy.15 = bf16[1,512,1024]{2,1,0:T(8,128)(2,1)} copy(bf16[1,512,1024]{2,1,0:T(8,128)(2,1)S(1)} %get-tuple-element.18) | data formatting | bytes 2097152
  84.4 1.0 %copy.16 = bf16[1,512,1024]{2,1,0:T(8,128)(2,1)} copy(bf16[1,512,1024]{2,1,0:T(8,128)(2,1)S(1)} %get-tuple-element.19) | data formatting | bytes 2097152
Async XLA Ops:
  0.6 1.2 %copy-start = (bf16[1,512,1024]{2,1,0:T(8,128)(2,1)S(1)}, bf16[1,512,1024]{2,1,0:T(8,128)(2,1)}, u32[]{:S(2)}) copy-start(bf16[1,512,1024]{2,1,0:T(8,128)(2,1)} %wg_hbm.1) | copy-start | bytes 3145732
  1.9 1.2 %copy-start.1 = (bf16[1,512,1024]{2,1,0:T(8,128)(2,1)S(1)}, bf16[1,512,1024]{2,1,0:T(8,128)(2,1)}, u32[]{:S(2)}) copy-start(bf16[1,512,1024]{2,1,0:T(8,128)(2,1)} %wu_hbm.1) | copy-start | bytes 3145732
  3.1 0.9 %copy-start.2 = (bf16[128,8,128]{2,1,0:T(8,128)(2,1)S(1)}, bf16[128,8,128]{2,1,0:T(8,128)(2,1)}, u32[]{:S(2)}) copy-start(bf16[128,8,128]{2,1,0:T(8,128)(2,1)} %param.9) | copy-start | bytes 786436
  4.0 0.9 %copy-start.3 = (bf16[128,512]{1,0:T(8,128)(2,1)S(1)}, bf16[128,512]{1,0:T(8,128)(2,1)}, u32[]{:S(2)}) copy-start(bf16[128,512]{1,0:T(8,128)(2,1)} %tok_hbm.1) | copy-start | bytes 393220
  4.9 0.7 copy-start.4

commit v2 on v1

v2 whole, which is shorter than its diff:
```python
import functools
import math

import jax
import jax.numpy as jnp
from jax import lax
from jax.experimental import pallas as pl
from jax.experimental.pallas import tpu as pltpu
from jax.sharding import PartitionSpec as P

MESH = pl.DeviceIdType.MESH
BF16 = jnp.bfloat16
F32 = jnp.float32
CAP = 8
CHUNKS = 4
LIMIT = 60 * 1024 * 1024


def dot(a, b, dims=(((1,), (0,)), ((), ()))):
    return lax.dot_general(a, b, dims, preferred_element_type=F32)


def fold(i, n):
    c = i // 2
    return c if i % 2 == 0 else n - c if c else n // 2


def fold_vector(i, n):
    c, p = i >> 1, i & 1
    return jnp.where(p == 0, c, jnp.where(c == 0, n // 2, n - c))


def kernel(
    ny, nz, nx,
    tok_hbm, rout_hbm, wg_hbm, wu_hbm, cot_hbm,
    hid_out, dx_out, gg_out, gu_out,
    tok, rout, cot, w, send_d, recv_d, send_c, recv_c, send_h, recv_h, send_r, recv_r, sel_t, sel_pt,
    own_a, send_a, recv_a, send_f, recv_f, send_b, recv_b, d_pair,
    in_sem, w_sem, sd_sem, rd_sem, sc_sem, rc_sem, sh_sem, rh_sem, sr_sem, rr_sem,
    sa_sem, ra_sem, sf_sem, rf_sem, sb_sem, rb_sem, sg_sem, rg_sem, st_sem, rt_sem, sp_sem, rp_sem,
):
    experts = ny * nz
    tokens, features = tok.shape
    top = rout.shape[0]
    pairs, part = cot.shape
    group = experts // CHUNKS
    rows = group * CAP
    half = rows // 2
    me, mine = lax.axis_index("ep"), lax.axis_index("dp")
    y, z = me // nz, me % nz
    x, core = mine // 2, mine % 2
    partner = x * 2 + 1 - core

    def along_x(step):
        return lax.rem(x + step, nx) * 2 + core

    ahead, behind = along_x(1), along_x(nx - 1)

    def block_of(k):
        return along_x(k) if k < nx else lax.rem(x + k - nx, nx) * 2 + 1 - core

    def to_expert(o):
        dy, dz = fold(o // nz, ny), fold(o % nz, nz)
        return lax.rem(y + dy, ny) * nz + lax.rem(z + dz, nz)

    def to_source(o):
        dy, dz = fold(o // nz, ny), fold(o % nz, nz)
        return lax.rem(y + ny - dy, ny) * nz + lax.rem(z + nz - dz, nz)

    def wait_for(ref, sem):
        pltpu.make_async_copy(ref, ref, sem).wait()

    def remote(source, target, send_sem, recv_sem, device):
        pltpu.make_async_remote_copy(
            src_ref=source,
            dst_ref=target,
            send_sem=send_sem,
            recv_sem=recv_sem,
            device_id=device,
            device_id_type=MESH,
        ).start()

    def on_x(source, target, send_sem, recv_sem, device):
        remote(source, target, send_sem, recv_sem, (me, device))

    def span(c):
        first = max(1, c * group)
        return pl.ds(first, (c + 1) * group - first)

    def exchange(c, source, target, send_sem, recv_sem, where):
        for o in range(max(1, c * group), (c + 1) * group):
            remote(source.at[o], target.at[o], send_sem.at[c], recv_sem.at[c], (where(o), mine))

    def rows_of(ref, c):
        return ref[c * group : (c + 1) * group].reshape(rows, ref.shape[2])

    def put(source, target, c, value):
        value = value.astype(BF16).reshape(group, CAP, source.shape[2])
        source[c * group : (c + 1) * group] = value
        if c == 0:
            target[0:1] = value[0:1]

    small = [
        pltpu.make_async_copy(rout_hbm, rout, in_sem.at[0]),
        pltpu.make_async_copy(tok_hbm, tok, in_sem.at[1]),
        pltpu.make_async_copy(cot_hbm, cot, in_sem.at[2]),
    ]
    for copy in small:
        copy.start()
    barrier = pltpu.get_barrier_semaphore()
    for o in range(experts - 1, 0, -1):
        pl.semaphore_signal(barrier, inc=1, device_id=(to_expert(o), mine), device_id_type=MESH)
    for there in (ahead, behind, partner):
        pl.semaphore_signal(barrier, inc=1, device_id=(me, there), device_id_type=MESH)
    w_copies = []
    for k in range(2 * nx):
        at = pl.ds(pl.multiple_of(block_of(k) * part, part), part)
        for n, source in enumerate((wg_hbm, wu_hbm)):
            copy = pltpu.make_async_copy(source.at[0, :, at], w.at[k, :, pl.ds(n * part, part)], w_sem.at[k, n])
            copy.start()
            w_copies.append(copy)

    before = (
        lax.broadcasted_iota(jnp.int32, (tokens, tokens), 0) < lax.broadcasted_iota(jnp.int32, (tokens, tokens), 1)
    ).astype(F32).astype(BF16)
    small[0].wait()
    routes = rout[...]

    def experts_of(c):
        row = lax.broadcasted_iota(jnp.int32, (rows, tokens), 0)
        o = row // CAP + c * group
        dy, dz = fold_vector(o // nz, ny), fold_vector(o % nz, nz)
        return ((y + dy) & (ny - 1)) * nz + ((z + dz) & (nz - 1)), row % CAP

    sels = []
    for c in range(CHUNKS):
        expert, slot = experts_of(c)
        hit = routes[0:1, :] == expert
        for k in range(1, top):
            hit = hit | (routes[k : k + 1, :] == expert)
        hit = hit.astype(F32)
        earlier = dot(hit.astype(BF16), before)
        sels.append(jnp.where(earlier == slot.astype(F32), hit, 0.0))
        if c == 0:
            small[1].wait()
        put(send_d, recv_d, c, dot(sels[c].astype(BF16), tok[...]))
    pl.semaphore_wait(barrier, experts + 2)
    for c in range(CHUNKS):
        exchange(c, send_d, recv_d, sd_sem, rd_sem, to_expert)

    spread = (
        lax.broadcasted_iota(jnp.int32, (tokens, pairs), 1) // top == lax.broadcasted_iota(jnp.int32, (tokens, pairs), 0)
    ).astype(F32).astype(BF16)
    named = dot(routes.astype(F32).astype(BF16), spread)
    place = lax.broadcasted_iota(jnp.int32, (top, pairs), 1) % top == lax.broadcasted_iota(jnp.int32, (top, pairs), 0)
    chosen = jnp.sum(jnp.where(place, named, 0.0), axis=0, keepdims=True)
    small[2].wait()
    for c in range(CHUNKS):
        expert, _ = experts_of(c)
        expanded = dot(sels[c].astype(BF16), spread)
        sel_pair = jnp.where(chosen == expert.astype(F32)[:, 0:1], expanded, 0.0)
        put(send_c, recv_c, c, dot(sel_pair.astype(BF16), cot[...]))
        sel_t[c] = sels[c].T.astype(BF16)
        sel_pt[c] = sel_pair.T.astype(BF16)
    for copy in w_copies:
        copy.wait()

    def project(c):
        wait_for(recv_d.at[span(c)], rd_sem.at[c])
        held = rows_of(recv_d, c)
        for k in (2, 1, 3, 0):
            send_a[c, k] = dot(held, w[nx + k]).astype(BF16)
        on_x(send_a.at[c], recv_a.at[c], sa_sem.at[c], ra_sem.at[c], partner)
        for k in (2, 1, 3, 0):
            own_a[c, k] = dot(held, w[k])
        exchange(c, send_c, recv_c, sc_sem, rc_sem, to_expert)

    low, high = pl.ds(0, half), pl.ds(half, half)

    def add_partner(c):
        wait_for(recv_a.at[c], ra_sem.at[c])
        send_f[c] = (own_a[c, 2] + recv_a[c, 2].astype(F32)).astype(BF16)
        on_x(send_f.at[c, low], recv_f.at[c, low], sf_sem.at[c, 0], rf_sem.at[c, 0], ahead)
        on_x(send_f.at[c, high], recv_f.at[c, high], sf_sem.at[c, 1], rf_sem.at[c, 1], behind)
        send_b[c, 0, half:] = (own_a[c, 1, half:] + recv_a[c, 1, half:].astype(F32)).astype(BF16)
        on_x(send_b.at[c, 0, high], recv_b.at[c, 0, high], sb_sem.at[c, 0], rb_sem.at[c, 0], ahead)
        send_b[c, 1, :half] = (own_a[c, 3, :half] + recv_a[c, 3, :half].astype(F32)).astype(BF16)
        on_x(send_b.at[c, 1, low], recv_b.at[c, 1, low], sb_sem.at[c, 1], rb_sem.at[c, 1], behind)

    def relay(c):
        wait_for(recv_f.at[c, low], rf_sem.at[c, 0])
        first = own_a[c, 1, :half] + recv_a[c, 1, :half].astype(F32) + recv_f[c, :half].astype(F32)
        send_b[c, 0, :half] = first.astype(BF16)
        on_x(send_b.at[c, 0, low], recv_b.at[c, 0, low], sb_sem.at[c, 2], rb_sem.at[c, 2], ahead)
        wait_for(recv_f.at[c, high], rf_sem.at[c, 1])
        second = own_a[c, 3, half:] + recv_a[c, 3, half:].astype(F32) + recv_f[c, half:].astype(F32)
        send_b[c, 1, half:] = second.astype(BF16)
        on_x(send_b.at[c, 1, high], recv_b.at[c, 1, high], sb_sem.at[c, 3], rb_sem.at[c, 3], behind)

    def activate(c):
        wait_for(recv_b.at[c, 0, high], rb_sem.at[c, 0])
        wait_for(recv_b.at[c, 1, low], rb_sem.at[c, 1])
        wait_for(recv_b.at[c, 0, low], rb_sem.at[c, 2])
        wait_for(recv_b.at[c, 1, high], rb_sem.at[c, 3])
        pre = own_a[c, 0] + recv_a[c, 0].astype(F32) + recv_b[c, 0].astype(F32) + recv_b[c, 1].astype(F32)
        gate_pre, up_pre = pre[:, :part], pre[:, part:]
        wait_for(recv_c.at[span(c)], rc_sem.at[c])
        upstream = rows_of(recv_c, c).astype(F32)
        s = jax.nn.sigmoid(gate_pre)
        d_gate = upstream * up_pre * s * (1.0 + gate_pre * (1.0 - s))
        d_up = upstream * gate_pre * s
        d_pair[c, 0] = jnp.concatenate([d_gate, d_up], axis=1).astype(BF16)
        on_x(d_pair.at[c, 0], d_pair.at[c, nx - 1], sg_sem.at[c, 0], rg_sem.at[c, 0], ahead)
        on_x(d_pair.at[c, 0], d_pair.at[c, 1], sg_sem.at[c, 1], rg_sem.at[c, 1], behind)
        on_x(d_pair.at[c, 0], d_pair.at[c, nx], sp_sem.at[c, 0], rp_sem.at[c, 0], partner)
        put(send_h, recv_h, c, gate_pre * s * up_pre)
        exchange(c, send_h, recv_h, sh_sem, rh_sem, to_source)

    def forward(c):
        wait_for(d_pair.at[c, 3], rg_sem.at[c, 0])
        on_x(d_pair.at[c, 3, low], d_pair.at[c, 2, low], st_sem.at[c, 0], rt_sem.at[c, 0], ahead)
        on_x(d_pair.at[c, 3], d_pair.at[c, nx + 3], sp_sem.at[c, 3], rp_sem.at[c, 3], partner)
        wait_for(d_pair.at[c, 1], rg_sem.at[c, 1])
        on_x(d_pair.at[c, 1, high], d_pair.at[c, 2, high], st_sem.at[c, 1], rt_sem.at[c, 1], behind)
        on_x(d_pair.at[c, 1], d_pair.at[c, nx + 1], sp_sem.at[c, 1], rp_sem.at[c, 1], partner)

    def forward_far(c):
        wait_for(d_pair.at[c, 2, low], rt_sem.at[c, 0])
        wait_for(d_pair.at[c, 2, high], rt_sem.at[c, 1])
        on_x(d_pair.at[c, 2], d_pair.at[c, nx + 2], sp_sem.at[c, 2], rp_sem.at[c, 2], partner)

    def give_back(c):
        total = jnp.zeros((rows, features), F32)
        for k in (0, 1, 3, nx, nx + 1, nx + 3, 2, nx + 2):
            if k >= nx:
                wait_for(d_pair.at[c, k], rp_sem.at[c, k - nx])
            total = total + dot(d_pair[c, k], w[k], (((1,), (1,)), ((), ())))
        put(send_r, recv_r, c, total)
        exchange(c, send_r, recv_r, sr_sem, rr_sem, to_source)

    stages = (project, add_partner, relay, activate, forward, forward_far, give_back)
    for step in range(CHUNKS + len(stages) - 1):
        for late, stage in enumerate(stages):
            if 0 <= step - late < CHUNKS:
                stage(step - late)

    held = jnp.concatenate([rows_of(recv_d, c) for c in range(CHUNKS)], axis=0)
    for k in range(2 * nx):
        both = d_pair[:, k].reshape(CHUNKS * rows, 2 * part)
        grad = dot(held, both, (((0,), (0,)), ((), ()))).astype(BF16)
        at = pl.ds(pl.multiple_of(block_of(k) * part, part), part)
        gg_out[0, :, at] = grad[:, :part]
        gu_out[0, :, at] = grad[:, part:]

    hidden = jnp.zeros((pairs, part), F32)
    for c in range(CHUNKS):
        wait_for(recv_h.at[span(c)], rh_sem.at[c])
        hidden = hidden + dot(sel_pt[c], rows_of(recv_h, c))
    hid_out[...] = hidden.astype(BF16)
    total = jnp.zeros((tokens, features), F32)
    for c in range(CHUNKS):
        wait_for(recv_r.at[span(c)], rr_sem.at[c])
        total = total + dot(sel_t[c], rows_of(recv_r, c))
    dx_out[...] = total.astype(BF16)

    for c in range(CHUNKS):
        wait_for(send_d.at[span(c)], sd_sem.at[c])
        wait_for(send_c.at[span(c)], sc_sem.at[c])
        wait_for(send_h.at[span(c)], sh_sem.at[c])
        wait_for(send_r.at[span(c)], sr_sem.at[c])
        wait_for(send_a.at[c], sa_sem.at[c])
        for n in range(2):
            wait_for(send_f.at[c, low], sf_sem.at[c, n])
            wait_for(d_pair.at[c, 0], sg_sem.at[c, n])
            wait_for(d_pair.at[c, 0, low], st_sem.at[c, n])
        for n in range(4):
            wait_for(send_b.at[c, 0, low], sb_sem.at[c, n])
            wait_for(d_pair.at[c, n], sp_sem.at[c, n])


def finish(*refs):
    count = (len(refs) - 1) // 2
    copies = [pltpu.make_async_copy(refs[n], refs[count + n], refs[-1].at[n]) for n in range(count)]
    for copy in copies:
        copy.start()
    for copy in copies:
        copy.wait()


def local(ny, nz, nx, tokens, routing, w_gate, w_up, cotangent):
    tok_rows, top = routing.shape
    features = tokens.shape[1]
    part = cotangent.shape[2]
    hidden_width = w_gate.shape[2]
    experts = ny * nz
    pairs = tok_rows * top
    rows = experts // CHUNKS * CAP
    flat = cotangent.reshape(pairs, part)
    hbm = pl.BlockSpec(memory_space=pltpu.HBM)
    vmem = pl.BlockSpec(memory_space=pltpu.VMEM)
    dma = pltpu.SemaphoreType.DMA
    by_slot = [pltpu.VMEM((experts, CAP, width), BF16) for width in (features, part, part, features) for _ in range(2)]
    shapes = ((pairs, part), (tok_rows, features), (1, features, hidden_width), (1, features, hidden_width))
    results = pl.pallas_call(
        functools.partial(kernel, ny, nz, nx),
        out_shape=tuple(pltpu.VMEM(shape, BF16) for shape in shapes),
        in_specs=[hbm] * 5,
        out_specs=(vmem,) * 4,
        scratch_shapes=[
            pltpu.VMEM((tok_rows, features), BF16),
            pltpu.VMEM((top, tok_rows), jnp.int32),
            pltpu.VMEM((pairs, part), BF16),
            pltpu.VMEM((2 * nx, features, 2 * part), BF16),
            *by_slot,
            pltpu.VMEM((CHUNKS, tok_rows, rows), BF16),
            pltpu.VMEM((CHUNKS, pairs, rows), BF16),
            pltpu.VMEM((CHUNKS, nx, rows, 2 * part), F32),
            pltpu.VMEM((CHUNKS, nx, rows, 2 * part), BF16),
            pltpu.VMEM((CHUNKS, nx, rows, 2 * part), BF16),
            pltpu.VMEM((CHUNKS, rows, 2 * part), BF16),
            pltpu.VMEM((CHUNKS, rows, 2 * part), BF16),
            pltpu.VMEM((CHUNKS, 2, rows, 2 * part), BF16),
            pltpu.VMEM((CHUNKS, 2, rows, 2 * part), BF16),
            pltpu.VMEM((CHUNKS, 2 * nx, rows, 2 * part), BF16),
            dma((3,)),
            dma((2 * nx, 2)),
            *[dma((CHUNKS,))] * 10,
            *[dma((CHUNKS, 2))] * 2,
            *[dma((CHUNKS, 4))] * 2,
            *[dma((CHUNKS, 2))] * 4,
            *[dma((CHUNKS, 4))] * 2,
        ],
        compiler_params=pltpu.CompilerParams(
            collective_id=0, has_side_effects=True, vmem_limit_bytes=LIMIT
        ),
        name="experts",
    )(tokens, routing.T, w_gate, w_up, flat)
    hidden, dx, gg, gu = pl.pallas_call(
        finish,
        out_shape=tuple(jax.ShapeDtypeStruct(shape, BF16) for shape in shapes),
        in_specs=[pl.BlockSpec(memory_space=pl.ANY)] * 4,
        out_specs=(hbm,) * 4,
        scratch_shapes=[dma((4,))],
        compiler_params=pltpu.CompilerParams(vmem_limit_bytes=1024 * 1024),
        name="finish",
    )(*results)
    return hidden.reshape(tok_rows, top, part), dx, gg, gu


def solution(mesh):
    experts, groups = mesh.shape["ep"], mesh.shape["dp"]
    ny = math.isqrt(experts)
    nz = experts // ny
    in_specs = (
        P("ep", "dp"),
        P("ep", None),
        P("ep", "dp", None),
        P("ep", "dp", None),
        P("ep", None, "dp"),
    )
    out_specs = (P("ep", None, "dp"), P("ep", "dp"), P("ep", "dp", None), P("ep", "dp", None))
    return jax.shard_map(
        functools.partial(local, ny, nz, groups // 2), mesh=mesh, in_specs=in_specs, out_specs=out_specs, check_vma=False
    )
```

time: 85.6 us -> 70.5 us (0.82)
  local copies, waits for them, and re-layouts: 8.28 us -> 0 us
  Pallas kernels: 76.4 us -> 69.7 us
    unnamed x14 -> x0, local copies, waits for them, and re-layouts: 8.28 us -> none
    pallas_call x1 -> x2, Pallas kernels: 76.4 us -> 69.7 us  [the longest x1 68.2 us: local(): pl.pallas_call(functools.partial(kernel, ny, nz, nx), out_shape=tuple((pl...]
where the time goes in v2:
time: 70.5 us; the launch traced here: 70.3 us
  Pallas kernels  69.7 us (99%)
    pallas_call x1, Pallas kernels, local(): pl.pallas_call(functools.partial(kernel, ny, nz, nx), out_shape=tuple((pl...  68.2 us
    pallas_call x1, Pallas kernels, local(): pl.pallas_call(finish, out_shape=tuple((jax.ShapeDtypeStruct(shape, BF16)...  1.48 us

profile of v2, /device:TPU:1, one launch (start us, length us, event | category | flops | bytes accessed | tf_op | source)
XLA Modules:
  0.0 70.3 jit_solution(14347536526959789525)
XLA Ops:
  0.6 68.2 %experts.1 = (bf16[1024,128]{1,0:T(8,128)(2,1)S(1)}, bf16[128,512]{1,0:T(8,128)(2,1)S(1)}, bf16[1,512,1024]{2,1,0:T(8,128)(2,1)S(1)}, bf16[1,512,1024]{2,1,0:T(8,128)(2,1)S(1)}) custom-call(bf16[128,512]{1,0:T(8,128)(2,1)} %tok_hbm.1, s32[8,128]{1,0:T(8,128)} %bitcast.4, bf16[1,512,1024]{2,1,0:T(8,128)(2,1)} %wg_hbm.1, bf16[1,512,1024]{2,1,0:T(8,128)(2,1)} %wu_hbm.1, ...), custom_call_target="tpu_custom_call" | custom-call | tf_op jit(solution)/shard_map/experts/pallas_call | solution.py:304
  68.9 1.5 %finish.1 = (bf16[1024,128]{1,0:T(8,128)(2,1)}, bf16[128,512]{1,0:T(8,128)(2,1)}, bf16[1,512,1024]{2,1,0:T(8,128)(2,1)}, bf16[1,512,1024]{2,1,0:T(8,128)(2,1)}) custom-call(bf16[1024,128]{1,0:T(8,128)(2,1)S(1)} %get-tuple-element.12.refs_0_, bf16[128,512]{1,0:T(8,128)(2,1)S(1)} %get-tuple-element.13.refs_1_, ...), custom_call_target="tpu_custom_call" | custom-call | tf_op jit(solution)/shard_map/finish/pallas_call | solution.py:338

commit v3 on v2

--- a/solution.py
+++ b/solution.py
@@ -20,14 +20,14 @@
     return lax.dot_general(a, b, dims, preferred_element_type=F32)
 
 
-def fold(i, n):
-    c = i // 2
-    return c if i % 2 == 0 else n - c if c else n // 2
-
-
-def fold_vector(i, n):
-    c, p = i >> 1, i & 1
-    return jnp.where(p == 0, c, jnp.where(c == 0, n // 2, n - c))
+def offsets_of(ny, nz):
+    def hops(n, size):
+        return min(n, size - n)
+
+    found = [(dy, dz) for dy in range(ny) for dz in range(nz)]
+    found.sort(key=lambda d: (hops(d[0], ny) + hops(d[1], nz), abs(hops(d[0], ny) - hops(d[1], nz)), d))
+    group = len(found) // CHUNKS
+    return [d for c in reversed(range(CHUNKS)) for d in found[c * group : (c + 1) * group]]
 
 
 def kernel(
@@ -59,12 +59,15 @@
     def block_of(k):
         return along_x(k) if k < nx else lax.rem(x + k - nx, nx) * 2 + 1 - core
 
+    offsets = offsets_of(ny, nz)
+    own = offsets.index((0, 0))
+
     def to_expert(o):
-        dy, dz = fold(o // nz, ny), fold(o % nz, nz)
+        dy, dz = offsets[o]
         return lax.rem(y + dy, ny) * nz + lax.rem(z + dz, nz)
 
     def to_source(o):
-        dy, dz = fold(o // nz, ny), fold(o % nz, nz)
+        dy, dz = offsets[o]
         return lax.rem(y + ny - dy, ny) * nz + lax.rem(z + nz - dz, nz)
 
     def wait_for(ref, sem):
@@ -84,11 +87,11 @@
         remote(source, target, send_sem, recv_sem, (me, device))
 
     def span(c):
-        first = max(1, c * group)
+        first = c * group + (c * group == own)
         return pl.ds(first, (c + 1) * group - first)
 
     def exchange(c, source, target, send_sem, recv_sem, where):
-        for o in range(max(1, c * group), (c + 1) * group):
+        for o in range(c * group + (c * group == own), (c + 1) * group):
             remote(source.at[o], target.at[o], send_sem.at[c], recv_sem.at[c], (where(o), mine))
 
     def rows_of(ref, c):
@@ -97,8 +100,8 @@
     def put(source, target, c, value):
         value = value.astype(BF16).reshape(group, CAP, source.shape[2])
         source[c * group : (c + 1) * group] = value
-        if c == 0:
-            target[0:1] = value[0:1]
+        if c * group == own:
+            target[own : own + 1] = value[0:1]
 
     small = [
         pltpu.make_async_copy(rout_hbm, rout, in_sem.at[0]),
@@ -108,7 +111,9 @@
     for copy in small:
         copy.start()
     barrier = pltpu.get_barrier_semaphore()
-    for o in range(experts - 1, 0, -1):
+    for o in range(experts):
+        if o == own:
+            continue
         pl.semaphore_signal(barrier, inc=1, device_id=(to_expert(o), mine), device_id_type=MESH)
     for there in (ahead, behind, partner):
         pl.semaphore_signal(barrier, inc=1, device_id=(me, there), device_id_type=MESH)
@@ -128,8 +133,10 @@
 
     def experts_of(c):
         row = lax.broadcasted_iota(jnp.int32, (rows, tokens), 0)
-        o = row // CAP + c * group
-        dy, dz = fold_vector(o // nz, ny), fold_vector(o % nz, nz)
+        dy, dz = jnp.zeros_like(row), jnp.zeros_like(row)
+        for n, (ahead_y, ahead_z) in enumerate(offsets[c * group : (c + 1) * group]):
+            here = row // CAP == n
+            dy, dz = jnp.where(here, ahead_y, dy), jnp.where(here, ahead_z, dz)
         return ((y + dy) & (ny - 1)) * nz + ((z + dz) & (nz - 1)), row % CAP
 
     sels = []
@@ -257,17 +264,10 @@
         wait_for(recv_h.at[span(c)], rh_sem.at[c])
         hidden = hidden + dot(sel_pt[c], rows_of(recv_h, c))
     hid_out[...] = hidden.astype(BF16)
-    total = jnp.zeros((tokens, features), F32)
-    for c in range(CHUNKS):
-        wait_for(recv_r.at[span(c)], rr_sem.at[c])
-        total = total + dot(sel_t[c], rows_of(recv_r, c))
-    dx_out[...] = total.astype(BF16)
-
     for c in range(CHUNKS):
         wait_for(send_d.at[span(c)], sd_sem.at[c])
         wait_for(send_c.at[span(c)], sc_sem.at[c])
         wait_for(send_h.at[span(c)], sh_sem.at[c])
-        wait_for(send_r.at[span(c)], sr_sem.at[c])
         wait_for(send_a.at[c], sa_sem.at[c])
         for n in range(2):
             wait_for(send_f.at[c, low], sf_sem.at[c, n])
@@ -276,6 +276,14 @@
         for n in range(4):
             wait_for(send_b.at[c, 0, low], sb_sem.at[c, n])
             wait_for(d_pair.at[c, n], sp_sem.at[c, n])
+
+    total = jnp.zeros((tokens, features), F32)
+    for c in range(CHUNKS):
+        wait_for(recv_r.at[span(c)], rr_sem.at[c])
+        total = total + dot(sel_t[c], rows_of(recv_r, c))
+    dx_out[...] = total.astype(BF16)
+    for c in range(CHUNKS):
+        wait_for(send_r.at[span(c)], sr_sem.at[c])
 
 
 def finish(*refs):

time: 70.5 us -> 68.8 us (0.976)
  Pallas kernels: 69.7 us -> 68 us
    pallas_call x1, Pallas kernels: 68.2 us -> 66.5 us  [local(): pl.pallas_call(functools.partial(kernel, ny, nz, nx), out_shape=tuple((pl...]
where the time goes in v3:
time: 68.8 us; the launch traced here: 68.6 us
  Pallas kernels  68 us (99%)
    pallas_call x1, Pallas kernels, local(): pl.pallas_call(functools.partial(kernel, ny, nz, nx), out_shape=tuple((pl...  66.5 us
    pallas_call x1, Pallas kernels, local(): pl.pallas_call(finish, out_shape=tuple((jax.ShapeDtypeStruct(shape, BF16)...  1.48 us

profile of v3, /device:TPU:1, one launch (start us, length us, event | category | flops | bytes accessed | tf_op | source)
XLA Modules:
  0.0 68.6 jit_solution(17268231230514409406)
XLA Ops:
  0.6 66.5 %experts.1 = (bf16[1024,128]{1,0:T(8,128)(2,1)S(1)}, bf16[128,512]{1,0:T(8,128)(2,1)S(1)}, bf16[1,512,1024]{2,1,0:T(8,128)(2,1)S(1)}, bf16[1,512,1024]{2,1,0:T(8,128)(2,1)S(1)}) custom-call(bf16[128,512]{1,0:T(8,128)(2,1)} %tok_hbm.1, s32[8,128]{1,0:T(8,128)} %bitcast.4, bf16[1,512,1024]{2,1,0:T(8,128)(2,1)} %wg_hbm.1, bf16[1,512,1024]{2,1,0:T(8,128)(2,1)} %wu_hbm.1, ...), custom_call_target="tpu_custom_call" | custom-call | tf_op jit(solution)/shard_map/experts/pallas_call | solution.py:312
  67.1 1.5 %finish.1 = (bf16[1024,128]{1,0:T(8,128)(2,1)}, bf16[128,512]{1,0:T(8,128)(2,1)}, bf16[1,512,1024]{2,1,0:T(8,128)(2,1)}, bf16[1,512,1024]{2,1,0:T(8,128)(2,1)}) custom-call(bf16[1024,128]{1,0:T(8,128)(2,1)S(1)} %get-tuple-element.12.refs_0_, bf16[128,512]{1,0:T(8,128)(2,1)S(1)} %get-tuple-element.13.refs_1_, ...), custom_call_target="tpu_custom_call" | custom-call | tf_op jit(solution)/shard_map/finish/pallas_call | solution.py:346
